TPU v7x, 512 devices: a whole 4x8x8 slice. The times are simulated.
512 devices in a mesh: gx: 32 (over x_lo, y, core), row: 16 (over x_hi, z).
Axes of the slice: x: 4 (x_hi: 2, x_lo: 2; x = x_hi * 2 + x_lo), y: 8, z: 8, core: 2. Of those that a mesh axis runs over, the one named last changes fastest.
Arguments:
- test_vectors: float32 [2, 5, 64, 256, 128], P(None, None, 'gx', 'row')
- base_coeffs: float32 [101, 64, 256], P(None, 'gx', 'row'), as said below
- panel_set: float32 [512, 10, 10], P(('gx', 'row')), as said below
- owner_index: int32 [1], replicated, may hold values from 0 to 511
Outputs:
- basis: float32 [2, 5, 64, 128, 256], P(None, None, 'gx', 'row')
Inputs may be any that keep to these rules, and one draw needn't show every extreme that they name: `owner_index`: the index, with gx slowest, of the device whose panel this window uses. `panel_set`: panels are nonsingular. `base_coeffs`: viscosities are positive.
All inputs are finite; a program needn't handle non-finite values.
Results may differ from a plain program's by a relative error of at most 0.0003.
Values sent between devices are 32-bit elements; how exact they have to be, the bound alone decides.
No kernel may reach another device: no remote copies, remote signals or barrier semaphores. Data moves between devices by JAX's collectives and lax.ppermute only.
A program may use at most 64 MiB of HBM per device.

v0:
```python
import math
import jax
import jax.numpy as jnp
from jax import lax
from jax.sharding import PartitionSpec as P

STEPS = 2


def spread(value, axis, source):
    kept = jnp.where(lax.axis_index(axis) == source, value, 0).astype(value.dtype)
    return lax.psum(kept, axis)


def with_halo(block, sides, width):
    for axis, dim in sides:
        count = lax.axis_size(axis)
        forward = [(i, i + 1) for i in range(count - 1)]
        backward = [(target, source) for source, target in forward]
        low = lax.ppermute(
            lax.slice_in_dim(block, block.shape[dim] - width, None, axis=dim), axis, forward
        )
        high = lax.ppermute(lax.slice_in_dim(block, 0, width, axis=dim), axis, backward)
        block = jnp.concatenate([low, block, high], axis=dim)
    return block


def advance(padded, coeffs):
    n_var = padded.shape[1]
    n_pair = n_var * n_var
    advect = coeffs[: 3 * n_pair].reshape((3, n_var, n_var) + coeffs.shape[1:])
    reaction = coeffs[3 * n_pair : 4 * n_pair].reshape((n_var, n_var) + coeffs.shape[1:])
    viscous = coeffs[4 * n_pair]
    fluxes = jnp.einsum("djixr,kjxrt->dkixrt", advect, padded, precision=lax.Precision.HIGHEST)
    centre = padded[:, :, 1:-1, 1:-1]
    stream = fluxes[0, :, :, 2:, 1:-1] - fluxes[0, :, :, :-2, 1:-1]
    radial = fluxes[1, :, :, 1:-1, 2:] - fluxes[1, :, :, 1:-1, :-2]
    beside_all = fluxes[2, :, :, 1:-1, 1:-1]
    azimuth = jnp.roll(beside_all, -1, axis=4) - jnp.roll(beside_all, 1, axis=4)
    neighbours = (
        padded[:, :, 2:, 1:-1]
        + padded[:, :, :-2, 1:-1]
        + padded[:, :, 1:-1, 2:]
        + padded[:, :, 1:-1, :-2]
    )
    neighbours = neighbours + jnp.roll(centre, -1, axis=4) + jnp.roll(centre, 1, axis=4)
    source = jnp.einsum(
        "jixr,kjxrt->kixrt", reaction[:, :, 1:-1, 1:-1], centre, precision=lax.Precision.HIGHEST
    )
    return (
        centre
        + stream
        + radial
        + azimuth
        + viscous[1:-1, 1:-1, None] * (neighbours - 6.0 * centre)
        + source
    )


def body(test_vectors, base_coeffs, panel_set, owner_index):
    panel_now = spread(panel_set[0], ("gx", "row"), owner_index[0])
    field = test_vectors
    count_x = lax.axis_size("gx")
    count_r = lax.axis_size("row")
    wide_x = field.shape[2]
    wide_r = field.shape[3]
    n_theta = field.shape[4]
    n_var = field.shape[1]
    n_vec = field.shape[0]
    coeff_rim = with_halo(base_coeffs, (("gx", 1), ("row", 2)), 1)
    for repeat in range(STEPS):
        padded = with_halo(field, (("gx", 2), ("row", 3)), 1)
        field = advance(padded, coeff_rim)
    sketch = jnp.dot(panel_now, field.reshape(n_vec * n_var, -1), precision=lax.Precision.HIGHEST)
    first = sketch[:n_var]
    second = sketch[n_var:]
    norm_one = lax.psum(jnp.sum(first * first), ("gx", "row"))
    inv_one = 1.0 / jnp.sqrt(norm_one)
    unit_one = first * inv_one
    projection = lax.psum(jnp.sum(unit_one * second), ("gx", "row"))
    remainder = second - projection * unit_one
    norm_two = lax.psum(jnp.sum(remainder * remainder), ("gx", "row"))
    inv_two = 1.0 / jnp.sqrt(norm_two)
    scale = math.sqrt(n_var * wide_x * count_x * wide_r * count_r * n_theta)
    weight_one = scale * inv_one
    weight_two = scale * inv_two
    weight_mix = -scale * inv_two * projection * inv_one
    block_shape = (n_var, wide_x, wide_r, n_theta)
    column_one = first.reshape(block_shape)
    column_two = second.reshape(block_shape)
    basis_local = jnp.stack(
        [weight_one * column_one, weight_two * column_two + weight_mix * column_one]
    )
    return lax.all_to_all(
        basis_local.transpose(0, 1, 2, 4, 3), "row", split_axis=3, concat_axis=4, tiled=True
    )


def solution(mesh):
    placed = (
        P(None, None, "gx", "row", None),
        P(None, "gx", "row"),
        P(("gx", "row"), None, None),
        P(),
    )
    return jax.shard_map(
        body,
        mesh=mesh,
        in_specs=placed,
        out_specs=P(None, None, "gx", "row", None),
        check_vma=False,
    )
```

profile of v0, /device:TPU:2, one launch (start us, length us, event | category | flops | bytes accessed | tf_op | source)
XLA Modules:
  0.0 481.5 jit_solution(10872169300837984554)
XLA Ops:
  1.1 1.9 collective-permute-start
  3.1 5.8 %collective-permute-start.1 = (f32[2,5,1,16,128]{4,1,0,3,2:T(8,128)S(1)}, f32[2,5,1,16,128]{4,1,0,3,2:T(8,128)S(1)}, u32[]{:S(2)}, u32[]{:S(2)}) collective-permute-start(f32[2,5,1,16,128]{4,1,0,3,2:T(8,128)S(1)} %get-tuple-element.29), channel_id=1, source_target_pairs={{16,0},{32,16},{48,32},{64,48},{80,64},{96,80},{112,96},{128,112},... | collective-permute-start | bytes 245768 | tf_op jit(solution)/shard_map/ppermute | solution.py:23
  9.5 1.9 collective-permute-start.4
  11.4 5.8 %collective-permute-start.5 = (f32[101,1,16]{0,2,1:T(8,128)S(1)}, f32[101,1,16]{0,2,1:T(8,128)S(1)}, u32[]{:S(2)}, u32[]{:S(2)}) collective-permute-start(f32[101,1,16]{0,2,1:T(8,128)S(1)} %get-tuple-element.33), channel_id=1, source_target_pairs={{16,0},{32,16},{48,32},{64,48},{80,64},{96,80},{112,96},{128,112},... | collective-permute-start | bytes 19400 | tf_op jit(solution)/shard_map/ppermute | solution.py:23
  18.6 4.3 collective-permute-start.6
  22.8 1.3 collective-permute-start.7
  24.2 105.0 %psum.28 = f32[10,10]{1,0:T(8,128)S(1)} all-reduce(f32[10,10]{1,0:T(8,128)S(1)} %fusion.42), channel_id=1, replica_groups=mesh['gx'=32,'row'=16] {'gx','row'}, use_global_device_ids=true, to_apply=%region_0.1 | all-reduce | flops 100 | bytes 800 | tf_op jit(solution)/shard_map/psum | solution.py:12
  129.4 2.5 collective-permute-start.2
  131.9 1.3 collective-permute-start.3
  134.7 3.0 collective-permute-done.3
  137.7 1.5 convolution_bitcast_fusion.1
  140.2 1.9 collective-permute-start.8
  142.1 5.8 %collective-permute-start.9 = (f32[2,5,1,16,128]{4,1,0,3,2:T(8,128)S(1)}, f32[2,5,1,16,128]{4,1,0,3,2:T(8,128)S(1)}, u32[]{:S(2)}, u32[]{:S(2)}) collective-permute-start(f32[2,5,1,16,128]{4,1,0,3,2:T(8,128)S(1)} %get-tuple-element.20), channel_id=1, source_target_pairs={{16,0},{32,16},{48,32},{64,48},{80,64},{96,80},{112,96},{128,112},... | collective-permute-start | bytes 245768 | tf_op jit(solution)/shard_map/ppermute | solution.py:23
  148.6 1.8 collective-permute-done.9
  150.4 2.2 collective-permute-start.10
  154.2 4.2 collective-permute-done.11
  158.4 1.5 convolution_bitcast_fusion
  162.0 105.2 %psum.29 = f32[]{:T(128)} all-reduce(f32[]{:T(128)} %multiply_reduce_fusion.2), channel_id=1, replica_groups=mesh['gx'=32,'row'=16] {'gx','row'}, use_global_device_ids=true, to_apply=%region_2.3 | all-reduce | flops 1 | bytes 8 | tf_op jit(solution)/shard_map/psum | solution.py:77
  268.5 93.0 %psum.30 = f32[]{:T(128)} all-reduce(f32[]{:T(128)} %multiply_reduce_fusion.1), channel_id=1, replica_groups=mesh['gx'=32,'row'=16] {'gx','row'}, use_global_device_ids=true, to_apply=%region_4.5 | all-reduce | flops 1 | bytes 8 | tf_op jit(solution)/shard_map/psum | solution.py:80
  361.6 1.3 multiply_bitcast_fusion
  362.9 95.2 %psum.31 = f32[]{:T(128)} all-reduce(f32[]{:T(128)} %get-tuple-element.10), channel_id=1, replica_groups=mesh['gx'=32,'row'=16] {'gx','row'}, use_global_device_ids=true, to_apply=%region_6.7 | all-reduce | flops 1 | bytes 8 | tf_op jit(solution)/shard_map/psum | solution.py:82
  460.8 1.8 reshape.70
  462.6 14.1 %all_to_all.18 = f32[16,1,2560]{2,1,0:T(1,128)S(1)} all-to-all(f32[16,1,2560]{2,1,0:T(1,128)S(1)} %reshape.70), channel_id=1, replica_groups=mesh['gx'=32,'row'=16] {'row'}, dimensions={0} | all-to-all | bytes 327680 | tf_op jit(solution)/shard_map/all_to_all | solution.py:94
  478.3 1.7 reshape.71
  (67 shorter events, 14.4 us)
Async XLA Ops:
  0.0 129.2 %copy-start = (f32[2,5,2,16,128]{4,3,2,1,0:T(8,128)S(1)}, f32[2,5,2,16,128]{4,3,2,1,0:T(8,128)}, u32[]{:S(2)}) copy-start(f32[2,5,2,16,128]{4,3,2,1,0:T(8,128)} %param.4) | copy-start | bytes 491524
  0.0 18.2 %copy-start.1 = (f32[101,2,16]{0,2,1:T(8,128)S(1)}, f32[101,2,16]{0,2,1:T(8,128)}, u32[]{:S(2)}) copy-start(f32[101,2,16]{0,2,1:T(8,128)} %param.5) | copy-start | bytes 38788
  0.0 24.1 %copy-start.2 = (f32[1,10,10]{2,0,1:T(1,128)S(1)}, f32[1,10,10]{2,0,1:T(1,128)}, u32[]{:S(2)}) copy-start(f32[1,10,10]{2,0,1:T(1,128)} %param.6) | copy-start | bytes 1204
  1.1 128.1 %collective-permute-start = (f32[2,5,1,16,128]{4,1,0,3,2:T(8,128)S(1)}, f32[2,5,1,16,128]{4,1,0,3,2:T(8,128)S(1)}, u32[]{:S(2)}, u32[]{:S(2)}) collective-permute-start(f32[2,5,1,16,128]{4,1,0,3,2:T(8,128)S(1)} %get-tuple-element.30), channel_id=1, source_target_pairs={{0,16},{16,32},{32,48},{48,64},{64,80},{80,96},{96,112},{112,128},... | collective-permute-start | bytes 245768 | tf_op jit(solution)/shard_map/ppermute | solution.py:20
  3.1 126.3 %collective-permute-start.1 = (f32[2,5,1,16,128]{4,1,0,3,2:T(8,128)S(1)}, f32[2,5,1,16,128]{4,1,0,3,2:T(8,128)S(1)}, u32[]{:S(2)}, u32[]{:S(2)}) collective-permute-start(f32[2,5,1,16,128]{4,1,0,3,2:T(8,128)S(1)} %get-tuple-element.29), channel_id=1, source_target_pairs={{16,0},{32,16},{48,32},{64,48},{80,64},{96,80},{112,96},{128,112},... | collective-permute-start | bytes 245768 | tf_op jit(solution)/shard_map/ppermute | solution.py:23
  9.5 8.6 %collective-permute-start.4 = (f32[101,1,16]{0,2,1:T(8,128)S(1)}, f32[101,1,16]{0,2,1:T(8,128)S(1)}, u32[]{:S(2)}, u32[]{:S(2)}) collective-permute-start(f32[101,1,16]{0,2,1:T(8,128)S(1)} %get-tuple-element.34), channel_id=1, source_target_pairs={{0,16},{16,32},{32,48},{48,64},{64,80},{80,96},{96,112},{112,128},... | collective-permute-start | bytes 19400 | tf_op jit(solution)/shard_map/ppermute | solution.py:20
  11.4 7.1 %collective-permute-start.5 = (f32[101,1,16]{0,2,1:T(8,128)S(1)}, f32[101,1,16]{0,2,1:T(8,128)S(1)}, u32[]{:S(2)}, u32[]{:S(2)}) collective-permute-start(f32[101,1,16]{0,2,1:T(8,128)S(1)} %get-tuple-element.33), channel_id=1, source_target_pairs={{16,0},{32,16},{48,32},{64,48},{80,64},{96,80},{112,96},{128,112},... | collective-permute-start | bytes 19400 | tf_op jit(solution)/shard_map/ppermute | solution.py:23
  18.6 110.6 %collective-permute-start.6 = (f32[101,4,1]{0,2,1:T(1,128)S(1)}, f32[101,4,1]{0,2,1:T(1,128)S(1)}, u32[]{:S(2)}, u32[]{:S(2)}) collective-permute-start(f32[101,4,1]{0,2,1:T(1,128)S(1)} %get-tuple-element.31), channel_id=1, source_target_pairs={{0,1},{1,2},{2,3},{3,4},{4,5},{5,6},{6,7},{7,8},{8,9},{9,10},{10,1... | collective-permute-start | bytes 4856 | tf_op jit(solution)/shard_map/ppermute | solution.py:20
  22.8 106.4 %collective-permute-start.7 = (f32[101,4,1]{0,2,1:T(1,128)S(1)}, f32[101,4,1]{0,2,1:T(1,128)S(1)}, u32[]{:S(2)}, u32[]{:S(2)}) collective-permute-start(f32[101,4,1]{0,2,1:T(1,128)S(1)} %get-tuple-element.32), channel_id=1, source_target_pairs={{1,0},{2,1},{3,2},{4,3},{5,4},{6,5},{7,6},{8,7},{9,8},{10,9},{11,1... | collective-permute-start | bytes 4856 | tf_op jit(solution)/shard_map/ppermute | solution.py:23
  129.4 5.3 %collective-permute-start.2 = (f32[2,5,4,1,128]{4,1,0,3,2:T(8,128)S(1)}, f32[2,5,4,1,128]{4,1,0,3,2:T(8,128)S(1)}, u32[]{:S(2)}, u32[]{:S(2)}) collective-permute-start(f32[2,5,4,1,128]{4,1,0,3,2:T(8,128)S(1)} %get-tuple-element.8), channel_id=1, source_target_pairs={{0,1},{1,2},{2,3},{3,4},{4,5},{5,6},{6,7},{7,8},{8,9},{9,10},{10,1... | collective-permute-start | bytes 61448 | tf_op jit(solution)/shard_map/ppermute | solution.py:20
  131.9 5.8 %collective-permute-start.3 = (f32[2,5,4,1,128]{4,1,0,3,2:T(8,128)S(1)}, f32[2,5,4,1,128]{4,1,0,3,2:T(8,128)S(1)}, u32[]{:S(2)}, u32[]{:S(2)}) collective-permute-start(f32[2,5,4,1,128]{4,1,0,3,2:T(8,128)S(1)} %get-tuple-element.7), channel_id=1, source_target_pairs={{1,0},{2,1},{3,2},{4,3},{5,4},{6,5},{7,6},{8,7},{9,8},{10,9},{11,1... | collective-permute-start | bytes 61448 | tf_op jit(solution)/shard_map/ppermute | solution.py:23
  140.2 8.4 %collective-permute-start.8 = (f32[2,5,1,16,128]{4,1,0,3,2:T(8,128)S(1)}, f32[2,5,1,16,128]{4,1,0,3,2:T(8,128)S(1)}, u32[]{:S(2)}, u32[]{:S(2)}) collective-permute-start(f32[2,5,1,16,128]{4,1,0,3,2:T(8,128)S(1)} %get-tuple-element.19), channel_id=1, source_target_pairs={{0,16},{16,32},{32,48},{48,64},{64,80},{80,96},{96,112},{112,128},... | collective-permute-start | bytes 245768 | tf_op jit(solution)/shard_map/ppermute | solution.py:20
  142.1 8.3 %collective-permute-start.9 = (f32[2,5,1,16,128]{4,1,0,3,2:T(8,128)S(1)}, f32[2,5,1,16,128]{4,1,0,3,2:T(8,128)S(1)}, u32[]{:S(2)}, u32[]{:S(2)}) collective-permute-start(f32[2,5,1,16,128]{4,1,0,3,2:T(8,128)S(1)} %get-tuple-element.20), channel_id=1, source_target_pairs={{16,0},{32,16},{48,32},{64,48},{80,64},{96,80},{112,96},{128,112},... | collective-permute-start | bytes 245768 | tf_op jit(solution)/shard_map/ppermute | solution.py:23
  150.4 3.8 collective-permute-start.10
  152.6 5.8 %collective-permute-start.11 = (f32[2,5,4,1,128]{4,1,0,3,2:T(8,128)S(1)}, f32[2,5,4,1,128]{4,1,0,3,2:T(8,128)S(1)}, u32[]{:S(2)}, u32[]{:S(2)}) collective-permute-start(f32[2,5,4,1,128]{4,1,0,3,2:T(8,128)S(1)} %get-tuple-element.5), channel_id=1, source_target_pairs={{1,0},{2,1},{3,2},{4,3},{5,4},{6,5},{7,6},{8,7},{9,8},{10,9},{11,1... | collective-permute-start | bytes 61448 | tf_op jit(solution)/shard_map/ppermute | solution.py:23
where the time goes:
time: 483 us; the launch traced here: 482 us
  blocking collectives  413 us (86%)
  starting transfers between devices  35.8 us (7%)
  local copies, waits for them, and re-layouts  11.6 us (2%)
  waiting for transfers between devices  10.1 us (2%)
    psum x1, blocking collectives, body(): norm_one = lax.psum(jnp.sum(first * first), ('gx', 'row'))  105 us
    psum x1, blocking collectives, spread(): return lax.psum(kept, axis)  105 us
    psum x1, blocking collectives, body(): norm_two = lax.psum(jnp.sum(remainder * remainder), ('gx', 'row'))  95.2 us
    psum x1, blocking collectives, body(): projection = lax.psum(jnp.sum(unit_one * second), ('gx', 'row'))  93 us
    ppermute x6, starting transfers between devices, with_halo(): lax.ppermute(lax.slice_in_dim(block, 0, width, axis=dim), axis, backward)  21.1 us
    ppermute x6, starting transfers between devices, with_halo(): lax.ppermute(lax.slice_in_dim(block, block.shape[dim] - width, None, axis...  14.7 us
    all_to_all x1, blocking collectives, body(): lax.all_to_all(basis_local.transpose(0, 1, 2, 4, 3), 'row', split_axis=3,...  14.1 us
  transfers between devices with their start and end apart: 12, of which 6 were waited for; matrix products, arithmetic and copies ran while one was open for 1% of the time, Pallas kernels for 0%

commit v1 on v0

--- a/solution.py
+++ b/solution.py
@@ -9,7 +9,13 @@
 
 def spread(value, axis, source):
     kept = jnp.where(lax.axis_index(axis) == source, value, 0).astype(value.dtype)
-    return lax.psum(kept, axis)
+
+    def do_the_sections(unit):
+        vec_out = lax.all_gather(unit, axis_name=axis)
+        frame_out = jnp.sum(vec_out, 0)
+        return frame_out
+
+    return do_the_sections(kept)
 
 
 def with_halo(block, sides, width):

time: 483 us -> 1760 us (3.64)
  blocking collectives: 413 us -> 1680 us
    all_gather x0 -> x1, blocking collectives: none -> 1220 us  [do_the_sections(): vec_out = lax.all_gather(unit, axis_name=axis)]
    psum x1, blocking collectives: 105 us -> 258 us  [body(): norm_one = lax.psum(jnp.sum(first * first), ('gx', 'row'))]
    psum x1 -> x0, blocking collectives: 105 us -> none  [spread(): return lax.psum(kept, axis)]
  transfers between devices with their start and end apart: 12 -> 12, of which waited for: 6 -> 6; matrix products, arithmetic and copies ran while one was open for 1% -> 0% of each run, Pallas kernels for 0% -> 0%
where the time goes in v1:
time: 1760 us
  blocking collectives  1680 us (95%)
  starting transfers between devices  34.6 us (2%)
  waiting for transfers between devices  18.6 us (1%)
    all_gather x1, blocking collectives, do_the_sections(): vec_out = lax.all_gather(unit, axis_name=axis)  1220 us
    psum x1, blocking collectives, body(): norm_one = lax.psum(jnp.sum(first * first), ('gx', 'row'))  258 us
    psum x1, blocking collectives, body(): norm_two = lax.psum(jnp.sum(remainder * remainder), ('gx', 'row'))  96.2 us
    psum x1, blocking collectives, body(): projection = lax.psum(jnp.sum(unit_one * second), ('gx', 'row'))  95.3 us
  transfers between devices with their start and end apart: 12, of which 6 were waited for; matrix products, arithmetic and copies ran while one was open for 0% of the time, Pallas kernels for 0%

profile of v1, /device:TPU:2, one launch (start us, length us, event | category | flops | bytes accessed | tf_op | source)
XLA Modules:
  0.0 1761.0 jit_solution(15314460530052584973)
XLA Ops:
  1.1 1.9 collective-permute-start
  3.0 5.8 collective-permute-start.1
  9.5 1.9 collective-permute-start.4
  11.4 5.8 collective-permute-start.5
  18.5 4.3 collective-permute-start.6
  22.8 1.3 collective-permute-start.7
  24.1 1217.8 %all_gather.4 = f32[512,10,10]{2,1,0:T(8,128)} all-gather(f32[1,10,10]{2,1,0:T(8,128)S(1)} %copy_select_fusion), channel_id=1, replica_groups=mesh['gx'=32,'row'=16] {'gx','row'}, dimensions={0}, use_global_device_ids=true | all-gather | bytes 205200 | tf_op jit(solution)/shard_map/all_gather | solution.py:14
  1241.9 2.8 reduce_sum.36
  1245.0 1.8 collective-permute-start.2
  1249.6 4.2 collective-permute-done.3
  1253.8 1.5 convolution_bitcast_fusion.1
  1256.3 1.9 collective-permute-start.8
  1258.2 5.8 collective-permute-start.9
  1264.7 9.0 collective-permute-done.9
  1273.7 1.6 collective-permute-start.10
  1276.9 4.2 collective-permute-done.11
  1281.2 1.5 convolution_bitcast_fusion
  1284.8 258.2 %psum.21 = f32[]{:T(128)} all-reduce(f32[]{:T(128)} %multiply_reduce_fusion.2), channel_id=1, replica_groups=mesh['gx'=32,'row'=16] {'gx','row'}, use_global_device_ids=true, to_apply=%region_2.3 | all-reduce | flops 1 | bytes 8 | tf_op jit(solution)/shard_map/psum | solution.py:83
  1544.3 95.3 %psum.22 = f32[]{:T(128)} all-reduce(f32[]{:T(128)} %multiply_reduce_fusion.1), channel_id=1, replica_groups=mesh['gx'=32,'row'=16] {'gx','row'}, use_global_device_ids=true, to_apply=%region_4.5 | all-reduce | flops 1 | bytes 8 | tf_op jit(solution)/shard_map/psum | solution.py:86
  1639.5 1.3 multiply_bitcast_fusion
  1640.9 96.2 %psum.23 = f32[]{:T(128)} all-reduce(f32[]{:T(128)} %get-tuple-element.10), channel_id=1, replica_groups=mesh['gx'=32,'row'=16] {'gx','row'}, use_global_device_ids=true, to_apply=%region_6.7 | all-reduce | flops 1 | bytes 8 | tf_op jit(solution)/shard_map/psum | solution.py:88
  1739.8 1.8 reshape.67
  1741.6 14.5 all_to_all.18
  1757.7 1.7 reshape.68
  (68 shorter events, 15.6 us)
Async XLA Ops:
  0.0 18.1 %copy-start.1 = (f32[101,2,16]{0,2,1:T(8,128)S(1)}, f32[101,2,16]{0,2,1:T(8,128)}, u32[]{:S(2)}) copy-start(f32[101,2,16]{0,2,1:T(8,128)} %param.5) | copy-start | bytes 38788
  0.0 18.1 %copy-start.2 = (f32[1,10,10]{2,0,1:T(1,128)S(1)}, f32[1,10,10]{2,0,1:T(1,128)}, u32[]{:S(2)}) copy-start(f32[1,10,10]{2,0,1:T(1,128)} %param.6) | copy-start | bytes 1204
  1.1 1243.7 %collective-permute-start = (f32[2,5,1,16,128]{4,1,0,3,2:T(8,128)S(1)}, f32[2,5,1,16,128]{4,1,0,3,2:T(8,128)S(1)}, u32[]{:S(2)}, u32[]{:S(2)}) collective-permute-start(f32[2,5,1,16,128]{4,1,0,3,2:T(8,128)S(1)} %get-tuple-element.30), channel_id=1, source_target_pairs={{0,16},{16,32},{32,48},{48,64},{64,80},{80,96},{96,112},{112,128},... | collective-permute-start | bytes 245768 | tf_op jit(solution)/shard_map/ppermute | solution.py:26
  3.0 1241.9 %collective-permute-start.1 = (f32[2,5,1,16,128]{4,1,0,3,2:T(8,128)S(1)}, f32[2,5,1,16,128]{4,1,0,3,2:T(8,128)S(1)}, u32[]{:S(2)}, u32[]{:S(2)}) collective-permute-start(f32[2,5,1,16,128]{4,1,0,3,2:T(8,128)S(1)} %get-tuple-element.29), channel_id=1, source_target_pairs={{16,0},{32,16},{48,32},{64,48},{80,64},{96,80},{112,96},{128,112},... | collective-permute-start | bytes 245768 | tf_op jit(solution)/shard_map/ppermute | solution.py:29
  9.5 8.6 collective-permute-start.4
  11.4 7.1 collective-permute-start.5
  18.5 1226.2 %collective-permute-start.6 = (f32[101,4,1]{0,2,1:T(1,128)S(1)}, f32[101,4,1]{0,2,1:T(1,128)S(1)}, u32[]{:S(2)}, u32[]{:S(2)}) collective-permute-start(f32[101,4,1]{0,2,1:T(1,128)S(1)} %get-tuple-element.31), channel_id=1, source_target_pairs={{0,1},{1,2},{2,3},{3,4},{4,5},{5,6},{6,7},{7,8},{8,9},{9,10},{10,1... | collective-permute-start | bytes 4856 | tf_op jit(solution)/shard_map/ppermute | solution.py:26
  22.8 1221.9 %collective-permute-start.7 = (f32[101,4,1]{0,2,1:T(1,128)S(1)}, f32[101,4,1]{0,2,1:T(1,128)S(1)}, u32[]{:S(2)}, u32[]{:S(2)}) collective-permute-start(f32[101,4,1]{0,2,1:T(1,128)S(1)} %get-tuple-element.32), channel_id=1, source_target_pairs={{1,0},{2,1},{3,2},{4,3},{5,4},{6,5},{7,6},{8,7},{9,8},{10,9},{11,1... | collective-permute-start | bytes 4856 | tf_op jit(solution)/shard_map/ppermute | solution.py:29
  1241.9 2.9 copy-start
  1245.0 4.7 collective-permute-start.2
  1246.8 7.0 collective-permute-start.3
  1256.3 8.4 collective-permute-start.8
  1258.2 15.5 collective-permute-start.9
  1273.7 3.2 collective-permute-start.10
  1275.4 5.8 collective-permute-start.11
